TPU v7x, 32 devices: a whole 2x2x4 slice. The times are simulated.
32 devices in a mesh: dp: 4 (over y, core), blk: 2 (over x), mp: 4 (over z).
Axes of the slice: x: 2, y: 2, z: 4, core: 2. Of those that a mesh axis runs over, the one named last changes fastest.
Arguments:
- queries: bfloat16 [4, 320, 2048], P('dp', 'blk', 'mp'), may hold values from -16 to 16
- keys: bfloat16 [4, 320, 2048], P('dp', 'blk', 'mp'), may hold values from -16 to 16
- values: bfloat16 [4, 320, 2048], P('dp', 'blk', 'mp'), may hold values from -6 to 6
- clip_ids: int32 [4, 320], P('dp', 'blk'), may hold values from 0 to 1, never falling along the last dimension, each value on 1 to 240 neighbouring positions
- w_out: bfloat16 [2048, 4096], P('mp'), may hold values from -0.125 to 0.125
- cotangent: bfloat16 [4, 320, 4096], P('dp', 'blk', 'mp'), may hold values from -6 to 6
Outputs:
- mixed: bfloat16 [4, 320, 4096], P('dp', 'blk', 'mp')
- d_queries: bfloat16 [4, 320, 2048], P('dp', 'blk', 'mp')
- d_keys: bfloat16 [4, 320, 2048], P('dp', 'blk', 'mp')
- d_values: bfloat16 [4, 320, 2048], P('dp', 'blk', 'mp')
- d_w_out: float32 [2048, 4096], P('mp', ('dp', 'blk'))
Inputs may be any that keep to these rules, and one draw needn't show every extreme that they name: `clip_ids`: each sequence holds clip 0 and then clip 1; each clip has at least 80 and at most 240 positions.
All inputs are finite; a program needn't handle non-finite values.
Results may differ from a plain program's by a relative error of at most 0.019.
Values may be sent and summed in bfloat16 or wider, within the bound.
A program may use at most 128 MiB of HBM per device.

v0:
```python
import jax
import jax.numpy as jnp
from jax import lax
from jax.sharding import PartitionSpec as P

HD = 128


NEG = -1e30


def seen_mask(q_pos, q_clip, k_pos, k_clip):
    return (k_pos[None, :] <= q_pos[:, None]) & (k_clip[None, :] == q_clip[:, None])


def per_device(queries, keys, values, clip_ids, w_out, cotangent):
    q_here = queries[0]
    k_here = keys[0]
    v_here = values[0]
    rows = q_here.shape[0]
    width = q_here.shape[1]
    heads = width // HD
    scale = HD ** (-0.5)
    first = lax.axis_index("blk") * rows
    q_pos = first + jnp.arange(rows, dtype=jnp.int32)
    clips_all = lax.all_gather(clip_ids[0], "blk", axis=0, tiled=True)
    clip_here = lax.dynamic_slice_in_dim(clips_all, first, rows, 0)
    qh = q_here.reshape(rows, heads, HD)
    kh = k_here.reshape(rows, heads, HD)
    vh = v_here.reshape(rows, heads, HD)
    k_piece = lax.all_gather(k_here, "blk", axis=0, tiled=True)
    v_piece = lax.all_gather(v_here, "blk", axis=0, tiled=True)
    count = k_piece.shape[0]
    k_pos = jnp.arange(count, dtype=jnp.int32)
    k_clip = clips_all
    allowed = seen_mask(q_pos, clip_here, k_pos, k_clip)
    peak = jnp.full((heads, rows), NEG, jnp.float32)
    accum = jnp.zeros((rows, heads, HD), jnp.float32)
    scores = (
        jnp.einsum(
            "qhd,khd->hqk",
            qh,
            k_piece.reshape(count, heads, HD),
            preferred_element_type=jnp.float32,
        )
        * scale
    )
    scores = jnp.where(allowed[None], scores, NEG)
    new_peak = jnp.maximum(peak, jnp.max(scores, axis=-1))
    factor = jnp.exp(peak - new_peak)
    probs = jnp.where(allowed[None], jnp.exp(scores - new_peak[:, :, None]), 0.0)
    total = jnp.sum(probs, axis=-1)
    v_block = v_piece.reshape(count, heads, HD).astype(jnp.float32)
    accum = accum * factor.T[:, :, None] + jnp.einsum(
        "hqk,khd->qhd",
        probs,
        v_block,
        precision=lax.Precision.HIGHEST,
        preferred_element_type=jnp.float32,
    )
    peak, total, accum = (new_peak, total, accum)
    lse = peak + jnp.log(total)
    attended = (accum / total.T[:, :, None]).astype(jnp.bfloat16).reshape(rows, width)
    partial_value = jnp.dot(attended, w_out, preferred_element_type=jnp.float32)
    mixed = lax.psum_scatter(partial_value, "mp", scatter_dimension=1, tiled=True).astype(
        jnp.bfloat16
    )
    cot_full = lax.all_gather(cotangent[0], "mp", axis=1, tiled=True)
    d_att = lax.dot_general(
        cot_full, w_out, (((1,), (1,)), ((), ())), preferred_element_type=jnp.float32
    ).astype(jnp.bfloat16)
    doh = d_att.reshape(rows, heads, HD)
    delta = jnp.sum(
        doh.astype(jnp.float32) * attended.reshape(rows, heads, HD).astype(jnp.float32), axis=-1
    )
    lse_all, delta_all = (
        lax.all_gather(lse.T, "blk", axis=0, tiled=True),
        lax.all_gather(delta, "blk", axis=0, tiled=True),
    )
    k_piece = lax.all_gather(k_here, "blk", axis=0, tiled=True)
    v_piece = lax.all_gather(v_here, "blk", axis=0, tiled=True)
    count = k_piece.shape[0]
    k_pos = jnp.arange(count, dtype=jnp.int32)
    k_clip = clips_all
    allowed = seen_mask(q_pos, clip_here, k_pos, k_clip)
    k_heads = k_piece.reshape(count, heads, HD)
    scores = jnp.einsum("qhd,khd->hqk", qh, k_heads, preferred_element_type=jnp.float32) * scale
    probs = jnp.where(
        allowed[None], jnp.exp(jnp.where(allowed[None], scores, NEG) - lse[:, :, None]), 0.0
    )
    d_probs = jnp.einsum(
        "qhd,khd->hqk", doh, v_piece.reshape(count, heads, HD), preferred_element_type=jnp.float32
    )
    d_scores = (probs * (d_probs - delta.T[:, :, None])).astype(jnp.bfloat16)
    dq_sum = jnp.einsum("hqk,khd->qhd", d_scores, k_heads, preferred_element_type=jnp.float32)
    q_piece = lax.all_gather(q_here, "blk", axis=0, tiled=True)
    do_piece = lax.all_gather(d_att, "blk", axis=0, tiled=True)
    count = q_piece.shape[0]
    p_pos = jnp.arange(count, dtype=jnp.int32)
    allowed = seen_mask(p_pos, clips_all, q_pos, clip_here)
    q_heads = q_piece.reshape(count, heads, HD)
    do_heads = do_piece.reshape(count, heads, HD)
    scores = jnp.einsum("qhd,khd->hqk", q_heads, kh, preferred_element_type=jnp.float32) * scale
    probs = jnp.where(
        allowed[None], jnp.exp(jnp.where(allowed[None], scores, NEG) - lse_all.T[:, :, None]), 0.0
    )
    dv_acc = jnp.einsum(
        "hqk,qhd->khd", probs.astype(jnp.bfloat16), do_heads, preferred_element_type=jnp.float32
    )
    d_probs = jnp.einsum("qhd,khd->hqk", do_heads, vh, preferred_element_type=jnp.float32)
    d_scores = (probs * (d_probs - delta_all.T[:, :, None])).astype(jnp.bfloat16)
    dk_acc = jnp.einsum("hqk,qhd->khd", d_scores, q_heads, preferred_element_type=jnp.float32)
    d_queries = (dq_sum * scale).astype(jnp.bfloat16).reshape(1, rows, width)
    d_keys = (dk_acc * scale).astype(jnp.bfloat16).reshape(1, rows, width)
    d_values = dv_acc.astype(jnp.bfloat16).reshape(1, rows, width)
    local_grad = lax.dot_general(
        attended, cot_full, (((0,), (0,)), ((), ())), preferred_element_type=jnp.float32
    )
    d_w_out = lax.psum_scatter(local_grad, ("dp", "blk"), scatter_dimension=1, tiled=True)
    return (mixed[None], d_queries, d_keys, d_values, d_w_out)


def solution(mesh):
    placed = (
        P("dp", "blk", "mp"),
        P("dp", "blk", "mp"),
        P("dp", "blk", "mp"),
        P("dp", "blk"),
        P("mp", None),
        P("dp", "blk", "mp"),
    )
    return jax.shard_map(
        per_device,
        mesh=mesh,
        in_specs=placed,
        out_specs=(
            P("dp", "blk", "mp"),
            P("dp", "blk", "mp"),
            P("dp", "blk", "mp"),
            P("dp", "blk", "mp"),
            P("mp", ("dp", "blk")),
        ),
        check_vma=False,
    )
```

profile of v0, /device:TPU:0, one launch (start us, length us, event | category | flops | bytes accessed | tf_op | source)
XLA Modules:
  0.0 185.6 jit_solution(8573655860317709714)
XLA Ops:
  7.2 0.7 all-gather.9.cloned.1.call-update
  8.0 1.0 reshape_squeeze.9
  8.9 8.1 %all-gather.1 = bf16[1,320,512]{2,1,0:T(8,128)(2,1)S(1)} all-gather(bf16[1,160,512]{2,1,0:T(8,128)(2,1)} %param.7), channel_id=3, replica_groups=mesh['dp'=4,'blk'=2,'mp'=4] {'blk'}, dimensions={1}, use_global_device_ids=true | all-gather | bytes 491520 | tf_op jit(solution)/shard_map/all_gather | solution.py:31
  17.1 6.3 %all-gather.2 = bf16[1,320,512]{2,1,0:T(8,128)(2,1)S(1)} all-gather(bf16[1,160,512]{2,1,0:T(8,128)(2,1)} %param.8), channel_id=4, replica_groups=mesh['dp'=4,'blk'=2,'mp'=4] {'blk'}, dimensions={1}, use_global_device_ids=true | all-gather | bytes 491520 | tf_op jit(solution)/shard_map/all_gather | solution.py:32
  23.4 1.2 dynamic-slice.1
  25.3 0.9 dynamic-update-slice
  26.2 4.3 %all-reduce = s32[320]{0:T(512)S(1)} all-reduce(s32[320]{0:T(512)S(1)} %dynamic-update-slice), channel_id=2, replica_groups=mesh['dp'=4,'blk'=2,'mp'=4] {'blk'}, use_global_device_ids=true, to_apply=%add | all-reduce | flops 320 | bytes 2560 | tf_op jit(solution)/shard_map/all_gather | solution.py:26
  30.6 0.1 fusion.54
  30.7 0.4 fusion.74
  31.1 0.5 fusion.31
  31.6 13.4 %all-gather.9.cloned.1.call-done = bf16[1,160,4096]{2,1,0:T(8,128)(2,1)} async-done(((bf16[1,160,1024]{2,1,0:T(8,128)(2,1)}), bf16[1,160,4096]{2,1,0:T(8,128)(2,1)}) %all-gather.9.cloned.1.call-update) | async-done | bytes 1310736 | tf_op jit(solution)/shard_map/all_gather | solution.py:68
  45.0 4.3 %fusion.21 = bf16[160,512]{1,0:T(8,128)(2,1)S(1)} fusion(bf16[512,4096]{1,0:T(8,128)(2,1)} %param.10, bf16[1,160,4096]{2,1,0:T(8,128)(2,1)} %all-gather.9.cloned.1.call-done), kind=kOutput, calls=%fused_computation.27 | convolution fusion | flops 671170560 | bytes 5668864 | tf_op jit(solution)/shard_map/dot_general | solution.py:69
  49.3 1.0 multiply_reduce_fusion
  50.3 2.5 %fusion.57 = f32[160,4096]{1,0:T(8,128)} fusion(bf16[512,4096]{1,0:T(8,128)(2,1)S(1)} %copy-done, bf16[160,4,128]{2,0,1:T(8,128)(2,1)S(1)} %get-tuple-element.10), kind=kOutput, calls=%fused_computation.63 | convolution fusion | flops 671088640 | bytes 6979584 | tf_op jit(solution)/shard_map/dot_general | solution.py:64
  52.8 4.5 %fusion.7 = f32[512,4096]{1,0:T(8,128)} fusion(bf16[1,160,4096]{2,1,0:T(8,128)(2,1)S(1)} %copy-done.1, bf16[160,4,128]{2,0,1:T(8,128)(2,1)S(1)} %get-tuple-element.10), kind=kOutput, calls=%fused_computation.11 | convolution fusion | flops 671088640 | bytes 9863168 | tf_op jit(solution)/shard_map/dot_general | solution.py:116
  57.4 0.9 copy-done.2
  58.4 0.1 copy-done.3
  58.6 6.0 %all-gather.4 = bf16[1,320,512]{2,1,0:T(8,128)(2,1)S(1)} all-gather(bf16[1,160,512]{2,1,0:T(8,128)(2,1)S(1)} %copy-done.4), channel_id=6, replica_groups=mesh['dp'=4,'blk'=2,'mp'=4] {'blk'}, dimensions={1}, use_global_device_ids=true | all-gather | bytes 491520 | tf_op jit(solution)/shard_map/all_gather | solution.py:96
  64.7 4.3 %all-gather.5 = f32[2,160,4]{1,2,0:T(4,128)S(1)} all-gather(f32[1,160,4]{1,2,0:T(4,128)S(1)} %get-tuple-element.5), channel_id=1, replica_groups=mesh['dp'=4,'blk'=2,'mp'=4] {'blk'}, dimensions={0}, use_global_device_ids=true | all-gather | bytes 7680 | tf_op jit(solution)/shard_map/all_gather | solution.py:77
  69.1 0.1 fusion.55
  69.2 0.4 fusion.4
  69.6 0.6 fusion.26
  70.3 0.7 reshape.160
  71.0 4.3 %all-gather.6 = f32[2,160,4]{1,2,0:T(4,128)S(1)} all-gather(f32[1,160,4]{1,2,0:T(4,128)S(1)} %bitcast.90), channel_id=1, replica_groups=mesh['dp'=4,'blk'=2,'mp'=4] {'blk'}, dimensions={0}, use_global_device_ids=true | all-gather | bytes 7680 | tf_op jit(solution)/shard_map/all_gather | solution.py:78
  75.5 6.0 %all_gather.32 = bf16[320,512]{1,0:T(8,128)(2,1)S(1)} all-gather(bf16[160,512]{1,0:T(8,128)(2,1)S(1)} %fusion.21), channel_id=1, replica_groups=mesh['dp'=4,'blk'=2,'mp'=4] {'blk'}, dimensions={0}, use_global_device_ids=true | all-gather | bytes 491520 | tf_op jit(solution)/shard_map/all_gather | solution.py:97
  81.5 0.3 fusion.25
  81.8 0.7 reshape.164
  82.6 0.4 fusion.27
  83.1 0.7 reshape.163
  83.8 20.2 %reduce-scatter.3.cloned.1.call-done = f32[160,1024]{1,0:T(8,128)} async-done(((f32[160,4096]{1,0:T(8,128)}), f32[160,1024]{1,0:T(8,128)}) %reduce-scatter.3.cloned.1.call-update) | async-done | bytes 655376 | tf_op jit(solution)/shard_map/reduce_scatter | solution.py:65
  104.0 1.9 convert_bitcast_fusion
  105.9 73.2 %reduce-scatter.5.cloned.1.call-done = f32[512,512]{1,0:T(8,128)} async-done(((f32[512,4096]{1,0:T(8,128)}), f32[512,512]{1,0:T(8,128)}) %reduce-scatter.5.cloned.1.call-update) | async-done | bytes 1048592 | tf_op jit(solution)/shard_map/reduce_scatter | solution.py:119
  (31 shorter events, 1.1 us)
Async XLA Ops:
  7.2 37.8 %all-gather.9.cloned.1.call-start = ((), (), s32[]{:S(2)}) async-start(), calls=%async_computation.4 | async-start | bytes 1638400 | tf_op jit(solution)/shard_map/all_gather | solution.py:68
  7.9 96.1 %reduce-scatter.3.cloned.1.call-start = ((), (), s32[]{:S(2)}) async-start(), calls=%async_computation.2 | async-start | bytes 3276800 | tf_op jit(solution)/shard_map/reduce_scatter | solution.py:65
  45.0 5.2 %copy-start = (bf16[512,4096]{1,0:T(8,128)(2,1)S(1)}, bf16[512,4096]{1,0:T(8,128)(2,1)}, u32[]{:S(2)}) copy-start(bf16[512,4096]{1,0:T(8,128)(2,1)} %param.10) | copy-start | bytes 12582916
  50.2 2.6 %copy-start.1 = (bf16[1,160,4096]{2,1,0:T(8,128)(2,1)S(1)}, bf16[1,160,4096]{2,1,0:T(8,128)(2,1)}, u32[]{:S(2)}) copy-start(bf16[1,160,4096]{2,1,0:T(8,128)(2,1)} %all-gather.9.cloned.1.call-done) | copy-start | bytes 3932164
  52.8 126.3 %reduce-scatter.5.cloned.1.call-start = ((), (), s32[]{:S(2)}) async-start(), calls=%async_computation.3 | async-start | bytes 9437184 | tf_op jit(solution)/shard_map/reduce_scatter | solution.py:119
  57.3 1.0 copy-start.2
  57.3 1.1 copy-start.3
  57.3 1.3 copy-start.4
Sparse Core Ops, SparseCore 0:
  9.6 35.3 all-gather.8
  52.9 51.0 reduce-scatter.2
  108.1 70.9 reduce-scatter.4
where the time goes:
time: 186 us
  waiting for transfers between devices  108 us (58%)
  blocking collectives  39.2 us (21%)
  between operations  14.5 us (8%)
  matrix products  14.3 us (8%)
  local copies, waits for them, and re-layouts  7.29 us (4%)
  other arithmetic  2.59 us (1%)
    reduce_scatter x1, waiting for transfers between devices, per_device(): lax.psum_scatter(local_grad, ('dp', 'blk'), scatter_dimension=1, tiled=True)  73.2 us
    reduce_scatter x1, waiting for transfers between devices, per_device(): lax.psum_scatter(partial_value, 'mp', scatter_dimension=1, tiled=True)  20.2 us
    all_gather x1, waiting for transfers between devices, per_device(): cot_full = lax.all_gather(cotangent[0], 'mp', axis=1, tiled=True)  13.4 us
    all_gather x1, blocking collectives, per_device(): k_piece = lax.all_gather(k_here, 'blk', axis=0, tiled=True)  8.07 us
    all_gather x1, blocking collectives, per_device(): v_piece = lax.all_gather(v_here, 'blk', axis=0, tiled=True)  6.27 us
    all_gather x1, blocking collectives, per_device(): do_piece = lax.all_gather(d_att, 'blk', axis=0, tiled=True)  5.98 us
    all_gather x1, blocking collectives, per_device(): q_piece = lax.all_gather(q_here, 'blk', axis=0, tiled=True)  5.98 us
    dot_general x1, matrix products, per_device(): lax.dot_general(attended, cot_full, (((0,), (0,)), ((), ())), preferred_e...  4.51 us
  transfers between devices with their start and end apart: 3, of which 3 were waited for; matrix products, arithmetic and copies ran while one was open for 8% of the time, Pallas kernels for 0%

commit v1 on v0

--- a/solution.py
+++ b/solution.py
@@ -1,12 +1,456 @@
+import functools
+
 import jax
 import jax.numpy as jnp
 from jax import lax
+from jax.experimental import pallas as pl
+from jax.experimental.pallas import tpu as pltpu
 from jax.sharding import PartitionSpec as P
 
 HD = 128
-
-
 NEG = -1e30
+MESH = pl.DeviceIdType.MESH
+NN = (((1,), (0,)), ((), ()))
+NT = (((1,), (1,)), ((), ()))
+TN = (((0,), (0,)), ((), ()))
+
+
+def dot(a, b, dims):
+    return lax.dot_general(a, b, dims, preferred_element_type=jnp.float32)
+
+
+def fused_kernel(
+    nd, nm, chunks,
+    q_ref, k_ref, v_ref, clip_ref, w_hbm, cot_ref,
+    mixed_ref, dq_ref, dk_ref, dv_ref, dw_ref,
+    w_ref, cot_full, cot_cols, att_all, kv_prev, clip_send, clip_prev,
+    p_own, p_prev, d_att, dkv_own, dkv_send, dkv_recv,
+    up_out, up_in, down_out, down_in,
+    w_sem, own_sem, kv_ssem, kv_rsem, ag_up_ssem, ag_dn_ssem, ag_rsem,
+    cc_ssem, cc_rsem, at_ssem, at_rsem,
+    up_ssem, up_rsem, dn_ssem, dn_rsem, dkv_ssem, dkv_rsem,
+):
+    nb = 2
+    d, b, m = lax.axis_index("dp"), lax.axis_index("blk"), lax.axis_index("mp")
+    me = d * nb + b
+    group = nd * nb
+    rows, width = q_ref.shape[1], q_ref.shape[2]
+    heads = width // HD
+    scale = HD ** (-0.5)
+    piece = cot_ref.shape[2]
+    half = piece // nb
+    part = piece // chunks
+
+    def remote(src, dst, ssem, rsem, device):
+        return pltpu.make_async_remote_copy(
+            src_ref=src, dst_ref=dst, send_sem=ssem, recv_sem=rsem,
+            device_id=device, device_id_type=MESH,
+        )
+
+    w_copy = pltpu.make_async_copy(w_hbm, w_ref, w_sem)
+    w_copy.start()
+
+    barrier = pltpu.get_barrier_semaphore()
+    for off in range(1, group):
+        other = lax.rem(me + off, group)
+        pl.semaphore_signal(
+            barrier, inc=1, device_id=(other // nb, lax.rem(other, nb), m), device_id_type=MESH
+        )
+
+    @pl.when(m > 0)
+    def _():
+        pl.semaphore_signal(barrier, inc=1, device_id=(d, b, m - 1), device_id_type=MESH)
+
+    @pl.when(m < nm - 1)
+    def _():
+        pl.semaphore_signal(barrier, inc=1, device_id=(d, b, m + 1), device_id_type=MESH)
+
+    clip_send[...] = jnp.zeros_like(clip_send)
+    clip_send[0:1, 0:rows] = clip_ref[...]
+    cot_full[m] = cot_ref[0]
+    pl.semaphore_wait(
+        barrier, group - 1 + jnp.where(m > 0, 1, 0) + jnp.where(m < nm - 1, 1, 0)
+    )
+
+    def kv_copies():
+        peer = (d, 1, m)
+        return (
+            remote(k_ref.at[0], kv_prev.at[0], kv_ssem.at[0], kv_rsem.at[0], peer),
+            remote(v_ref.at[0], kv_prev.at[1], kv_ssem.at[1], kv_rsem.at[1], peer),
+            remote(clip_send, clip_prev, kv_ssem.at[2], kv_rsem.at[2], peer),
+        )
+
+    def gather_up(shard):
+        return remote(
+            cot_full.at[shard], cot_full.at[shard], ag_up_ssem.at[shard], ag_rsem.at[shard],
+            (d, b, m + 1),
+        )
+
+    def gather_down(shard):
+        return remote(
+            cot_full.at[shard], cot_full.at[shard], ag_dn_ssem.at[shard], ag_rsem.at[shard],
+            (d, b, m - 1),
+        )
+
+    def column_copy(shard, to_b):
+        return remote(
+            cot_full.at[shard, :, pl.ds(to_b * half, half)], cot_cols.at[me],
+            cc_ssem.at[shard, to_b], cc_rsem.at[me], (shard, to_b, m),
+        )
+
+    def own_copy(to_b):
+        return pltpu.make_async_copy(
+            cot_full.at[d, :, pl.ds(to_b * half, half)], cot_cols.at[me], own_sem
+        )
+
+    def each_column(shard, away, here):
+        for to_b in range(nb):
+            is_me = jnp.logical_and(shard == d, b == to_b)
+
+            @pl.when(jnp.logical_not(is_me))
+            def _():
+                away(column_copy(shard, to_b))
+
+            @pl.when(is_me)
+            def _():
+                here(own_copy(to_b))
+
+    def start(copy):
+        copy.start()
+
+    @pl.when(m < nm - 1)
+    def _():
+        gather_up(m).start()
+
+    @pl.when(m > 0)
+    def _():
+        gather_down(m).start()
+
+    @pl.when(b == 0)
+    def _():
+        for copy in kv_copies():
+            copy.start()
+
+    each_column(m, start, start)
+
+    def gather_step(step):
+        @pl.when(m - step >= 0)
+        def _():
+            shard = m - step
+            gather_down(shard).wait_recv()
+
+            @pl.when(m < nm - 1)
+            def _():
+                gather_up(shard).start()
+
+            each_column(shard, start, start)
+
+        @pl.when(m + step < nm)
+        def _():
+            shard = m + step
+            gather_up(shard).wait_recv()
+
+            @pl.when(m > 0)
+            def _():
+                gather_down(shard).start()
+
+            each_column(shard, start, start)
+
+    row = lax.broadcasted_iota(jnp.int32, (rows, rows), 0)
+    col = lax.broadcasted_iota(jnp.int32, (rows, rows), 1)
+
+    def clip_masks(use_prev):
+        here = jnp.broadcast_to(clip_send[0:1, 0:rows], (rows, rows))
+        mine = jnp.sum(jnp.where(row == col, here, 0), axis=1, keepdims=True)
+        own = jnp.logical_and(col <= row, here == mine)
+        prev = None
+        if use_prev:
+            prev = jnp.broadcast_to(clip_prev[0:1, 0:rows], (rows, rows)) == mine
+        return own, prev
+
+    def forward(use_prev):
+        own, prev = clip_masks(use_prev)
+        for h in range(heads):
+            cols = pl.ds(h * HD, HD)
+            q = q_ref[0, :, cols]
+            s = jnp.where(own, dot(q, k_ref[0, :, cols], NT) * scale, NEG)
+            peak = jnp.max(s, axis=1, keepdims=True)
+            if use_prev:
+                t = jnp.where(prev, dot(q, kv_prev[0, :, cols], NT) * scale, NEG)
+                peak = jnp.maximum(peak, jnp.max(t, axis=1, keepdims=True))
+            e = jnp.exp(s - peak)
+            total = jnp.sum(e, axis=1, keepdims=True)
+            if use_prev:
+                f = jnp.exp(t - peak)
+                total = total + jnp.sum(f, axis=1, keepdims=True)
+            inverse = 1.0 / total
+            e = e * inverse
+            p_own[h] = e
+            att = dot(e.astype(jnp.bfloat16), v_ref[0, :, cols], NN)
+            if use_prev:
+                f = f * inverse
+                p_prev[h] = f
+                att = att + dot(f.astype(jnp.bfloat16), kv_prev[1, :, cols], NN)
+            att_all[me, :, cols] = att.astype(jnp.bfloat16)
+
+    @pl.when(b == 0)
+    def _():
+        forward(False)
+
+    gather_step(1)
+
+    @pl.when(b == 1)
+    def _():
+        for copy in kv_copies():
+            copy.wait_recv()
+        forward(True)
+
+    def att_copy(off):
+        other = lax.rem(me + off, group)
+        return remote(
+            att_all.at[me], att_all.at[me], at_ssem.at[off], at_rsem.at[me],
+            (other // nb, lax.rem(other, nb), m),
+        )
+
+    for off in range(1, group):
+        att_copy(off).start()
+
+    w_copy.wait()
+
+    def partial(dest, c):
+        at = pl.multiple_of(dest * piece + c * part, part)
+        return dot(att_all[me], w_ref[:, pl.ds(at, part)], NN)
+
+    def sum_up(dest, c):
+        return remote(
+            up_out.at[dest, c], up_in.at[dest, c], up_ssem.at[dest, c], up_rsem.at[dest, c],
+            (d, b, m + 1),
+        )
+
+    def sum_down(dest, c):
+        return remote(
+            down_out.at[dest, c], down_in.at[dest, c], dn_ssem.at[dest, c], dn_rsem.at[dest, c],
+            (d, b, m - 1),
+        )
+
+    def chain_step(step):
+        for c in range(chunks):
+            @pl.when(step >= m)
+            def _():
+                dest = nm - 1 - step + m
+                mine = partial(dest, c)
+
+                @pl.when(m == 0)
+                def _():
+                    up_out[dest, c] = mine.astype(jnp.bfloat16)
+
+                @pl.when(m > 0)
+                def _():
+                    sum_up(dest, c).wait_recv()
+                    up_out[dest, c] = (
+                        mine + up_in[dest, c].astype(jnp.float32)
+                    ).astype(jnp.bfloat16)
+
+                sum_up(dest, c).start()
+
+            @pl.when(step >= nm - 1 - m)
+            def _():
+                dest = step - (nm - 1 - m)
+                mine = partial(dest, c)
+
+                @pl.when(m == nm - 1)
+                def _():
+                    down_out[dest, c] = mine.astype(jnp.bfloat16)
+
+                @pl.when(m < nm - 1)
+                def _():
+                    sum_down(dest, c).wait_recv()
+                    down_out[dest, c] = (
+                        mine + down_in[dest, c].astype(jnp.float32)
+                    ).astype(jnp.bfloat16)
+
+                sum_down(dest, c).start()
+
+    for step in range(nm - 2):
+        chain_step(step)
+        gather_step(step + 2)
+
+    total = dot(cot_full[0], w_ref[:, 0:piece], NT)
+    for shard in range(1, nm):
+        total = total + dot(cot_full[shard], w_ref[:, shard * piece:(shard + 1) * piece], NT)
+    d_att[...] = total.astype(jnp.bfloat16)
+
+    def dkv_copy():
+        return remote(dkv_send, dkv_recv, dkv_ssem, dkv_rsem, (d, 0, m))
+
+    def backward(use_prev):
+        for h in range(heads):
+            cols = pl.ds(h * HD, HD)
+            do = d_att[:, cols]
+            q = q_ref[0, :, cols]
+            delta = jnp.sum(
+                do.astype(jnp.float32) * att_all[me, :, cols].astype(jnp.float32),
+                axis=1, keepdims=True,
+            )
+            e = p_own[h]
+            ds = (e * (dot(do, v_ref[0, :, cols], NT) - delta)).astype(jnp.bfloat16)
+            dq = dot(ds, k_ref[0, :, cols], NN)
+            dk = dot(ds, q, TN) * scale
+            dv = dot(e.astype(jnp.bfloat16), do, TN)
+            if use_prev:
+                f = p_prev[h]
+                dt = (f * (dot(do, kv_prev[1, :, cols], NT) - delta)).astype(jnp.bfloat16)
+                dq = dq + dot(dt, kv_prev[0, :, cols], NN)
+                dkv_send[0, :, cols] = (dot(dt, q, TN) * scale).astype(jnp.bfloat16)
+                dkv_send[1, :, cols] = dot(f.astype(jnp.bfloat16), do, TN).astype(jnp.bfloat16)
+                dk_ref[0, :, cols] = dk.astype(jnp.bfloat16)
+                dv_ref[0, :, cols] = dv.astype(jnp.bfloat16)
+            else:
+                dkv_own[0, :, cols] = dk
+                dkv_own[1, :, cols] = dv
+            dq_ref[0, :, cols] = (dq * scale).astype(jnp.bfloat16)
+
+    @pl.when(b == 0)
+    def _():
+        backward(False)
+
+    @pl.when(b == 1)
+    def _():
+        backward(True)
+        dkv_copy().start()
+
+    chain_step(nm - 2)
+
+    for off in range(1, group):
+        other = lax.rem(me + off, group)
+        peer = (other // nb, lax.rem(other, nb), m)
+        remote(
+            att_all.at[other], att_all.at[other], at_ssem.at[off], at_rsem.at[other], peer
+        ).wait_recv()
+        remote(
+            cot_cols.at[other], cot_cols.at[other], cc_ssem.at[0, 0], cc_rsem.at[other], peer
+        ).wait_recv()
+    own_copy(0).wait()
+    dw_ref[...] = dot(
+        att_all[...].reshape(group * rows, width), cot_cols[...].reshape(group * rows, half), TN
+    )
+
+    @pl.when(b == 0)
+    def _():
+        dkv_copy().wait_recv()
+        dk_ref[0] = (dkv_own[0] + dkv_recv[0].astype(jnp.float32)).astype(jnp.bfloat16)
+        dv_ref[0] = (dkv_own[1] + dkv_recv[1].astype(jnp.float32)).astype(jnp.bfloat16)
+
+    for c in range(chunks):
+        mine = partial(m, c)
+        at = slice(c * part, (c + 1) * part)
+
+        @pl.when(m > 0)
+        def _():
+            sum_up(m, c).wait_recv()
+
+        @pl.when(m < nm - 1)
+        def _():
+            sum_down(m, c).wait_recv()
+
+        @pl.when(m == 0)
+        def _():
+            mixed_ref[0, :, at] = (mine + down_in[m, c].astype(jnp.float32)).astype(jnp.bfloat16)
+
+        @pl.when(m == nm - 1)
+        def _():
+            mixed_ref[0, :, at] = (mine + up_in[m, c].astype(jnp.float32)).astype(jnp.bfloat16)
+
+        @pl.when(jnp.logical_and(m > 0, m < nm - 1))
+        def _():
+            mixed_ref[0, :, at] = (
+                mine + up_in[m, c].astype(jnp.float32) + down_in[m, c].astype(jnp.float32)
+            ).astype(jnp.bfloat16)
+
+    for shard in range(nm):
+        @pl.when(jnp.logical_and(m < nm - 1, shard <= m))
+        def _():
+            gather_up(shard).wait_send()
+
+        @pl.when(jnp.logical_and(m > 0, shard >= m))
+        def _():
+            gather_down(shard).wait_send()
+
+        for to_b in range(nb):
+            @pl.when(jnp.logical_not(jnp.logical_and(shard == d, b == to_b)))
+            def _():
+                column_copy(shard, to_b).wait_send()
+
+        for c in range(chunks):
+            @pl.when(shard > m)
+            def _():
+                sum_up(shard, c).wait_send()
+
+            @pl.when(shard < m)
+            def _():
+                sum_down(shard, c).wait_send()
+
+    for off in range(1, group):
+        att_copy(off).wait_send()
+
+    @pl.when(b == 0)
+    def _():
+        for copy in kv_copies():
+            copy.wait_send()
+
+    @pl.when(b == 1)
+    def _():
+        dkv_copy().wait_send()
+
+
+def fused(nd, nm, queries, keys, values, clip_ids, w_out, cotangent):
+    nb, chunks = 2, 2
+    group = nd * nb
+    _, rows, width = queries.shape
+    piece = cotangent.shape[2]
+    half, part = piece // nb, piece // chunks
+    heads = width // HD
+    lanes = -(-rows // 128) * 128
+    bf16, f32 = jnp.bfloat16, jnp.float32
+    dma = pltpu.SemaphoreType.DMA
+    vmem = pl.BlockSpec(memory_space=pltpu.VMEM)
+    return pl.pallas_call(
+        functools.partial(fused_kernel, nd, nm, chunks),
+        out_shape=(
+            jax.ShapeDtypeStruct((1, rows, piece), bf16),
+            jax.ShapeDtypeStruct((1, rows, width), bf16),
+            jax.ShapeDtypeStruct((1, rows, width), bf16),
+            jax.ShapeDtypeStruct((1, rows, width), bf16),
+            jax.ShapeDtypeStruct((width, half), f32),
+        ),
+        in_specs=[vmem] * 4 + [pl.BlockSpec(memory_space=pl.ANY), vmem],
+        out_specs=(vmem,) * 5,
+        scratch_shapes=[
+            pltpu.VMEM(w_out.shape, bf16),
+            pltpu.VMEM((nm, rows, piece), bf16),
+            pltpu.VMEM((group, rows, half), bf16),
+            pltpu.VMEM((group, rows, width), bf16),
+            pltpu.VMEM((2, rows, width), bf16),
+            pltpu.VMEM((8, lanes), jnp.int32),
+            pltpu.VMEM((8, lanes), jnp.int32),
+            pltpu.VMEM((heads, rows, rows), f32),
+            pltpu.VMEM((heads, rows, rows), f32),
+            pltpu.VMEM((rows, width), bf16),
+            pltpu.VMEM((2, rows, width), f32),
+            pltpu.VMEM((2, rows, width), bf16),
+            pltpu.VMEM((2, rows, width), bf16),
+            pltpu.VMEM((nm, chunks, rows, part), bf16),
+            pltpu.VMEM((nm, chunks, rows, part), bf16),
+            pltpu.VMEM((nm, chunks, rows, part), bf16),
+            pltpu.VMEM((nm, chunks, rows, part), bf16),
+            dma, dma, dma((3,)), dma((3,)), dma((nm,)), dma((nm,)), dma((nm,)),
+            dma((nm, nb)), dma((group,)), dma((group,)), dma((group,)),
+            dma((nm, chunks)), dma((nm, chunks)), dma((nm, chunks)), dma((nm, chunks)), dma, dma,
+        ],
+        compiler_params=pltpu.CompilerParams(
+            collective_id=0, has_side_effects=True, vmem_limit_bytes=48 * 1024 * 1024
+        ),
+    )(queries, keys, values, clip_ids, w_out, cotangent)
 
 
 def seen_mask(q_pos, q_clip, k_pos, k_clip):
@@ -129,8 +573,12 @@
         P("mp", None),
         P("dp", "blk", "mp"),
     )
+    nd, nb, nm = mesh.shape["dp"], mesh.shape["blk"], mesh.shape["mp"]
+    body = per_device
+    if nb == 2 and nd == nm:
+        body = functools.partial(fused, nd, nm)
     return jax.shard_map(
-        per_device,
+        body,
         mesh=mesh,
         in_specs=placed,
         out_specs=(

time: 186 us -> 56.6 us (0.30)
  waiting for transfers between devices: 108 us -> 0 us
  Pallas kernels: 0 us -> 47.6 us
  blocking collectives: 39.2 us -> 0 us
  matrix products: 14.3 us -> 0 us
  between operations: 14.5 us -> 0.66 us
  other arithmetic: 2.59 us -> 0 us
    reduce_scatter x2 -> x0, waiting for transfers between devices: 93.4 us -> none  [the longest x1 73.2 us: per_device(): lax.psum_scatter(local_grad, ('dp', 'blk'), scatter_dimension=1, tiled=True)]
    pallas_call x0 -> x1, Pallas kernels: none -> 47.6 us  [fused(): pl.pallas_call(functools.partial(fused_kernel, nd, nm, chunks), out_shape...]
    all_gather x7 -> x0, blocking collectives: 39.2 us -> none  [the longest x1 8.07 us: per_device(): k_piece = lax.all_gather(k_here, 'blk', axis=0, tiled=True)]
    dot_general x9 -> x0, matrix products: 14.3 us -> none  [the longest x1 4.51 us: per_device(): lax.dot_general(attended, cot_full, (((0,), (0,)), ((), ())), preferred_e...]
    all_gather x1 -> x0, waiting for transfers between devices: 13.4 us -> none  [per_device(): cot_full = lax.all_gather(cotangent[0], 'mp', axis=1, tiled=True)]
    unnamed x15, local copies, waits for them, and re-layouts: 3.46 us -> 8.08 us
    reshape x6 -> x0, local copies, waits for them, and re-layouts: 2.44 us -> none  [the longest x1 0.73 us: per_device(): d_keys = (dk_acc * scale).astype(jnp.bfloat16).reshape(1, rows, width)]
  transfers between devices with their start and end apart: 3 -> 0, of which waited for: 3 -> 0; matrix products, arithmetic and copies ran while one was open for 8% -> 0% of each run, Pallas kernels for 0% -> 0%
where the time goes in v1:
time: 56.6 us; the launch traced here: 56.4 us
  Pallas kernels  47.6 us (84%)
  local copies, waits for them, and re-layouts  8.08 us (14%)
  between operations  0.66 us (1%)
    pallas_call x1, Pallas kernels, fused(): pl.pallas_call(functools.partial(fused_kernel, nd, nm, chunks), out_shape...  47.6 us
    unnamed x15, local copies, waits for them, and re-layouts  8.08 us

profile of v1, /device:TPU:0, one launch (start us, length us, event | category | flops | bytes accessed | tf_op | source)
XLA Modules:
  0.0 56.4 jit_solution(2065461957817689318)
XLA Ops:
  0.6 0.0 copy-start
  0.6 1.0 %copy-done = bf16[1,160,1024]{2,1,0:T(8,128)(2,1)S(1)} copy-done((bf16[1,160,1024]{2,1,0:T(8,128)(2,1)S(1)}, bf16[1,160,1024]{2,1,0:T(8,128)(2,1)}, u32[]{:S(2)}) %copy-start) | copy-done | bytes 327704
  1.6 0.0 copy-start.1
  1.6 0.9 %copy-done.1 = bf16[1,160,512]{2,1,0:T(8,128)(2,1)S(1)} copy-done((bf16[1,160,512]{2,1,0:T(8,128)(2,1)S(1)}, bf16[1,160,512]{2,1,0:T(8,128)(2,1)}, u32[]{:S(2)}) %copy-start.1) | copy-done | bytes 163864
  2.5 0.0 copy-start.2
  2.5 0.9 %copy-done.2 = bf16[1,160,512]{2,1,0:T(8,128)(2,1)S(1)} copy-done((bf16[1,160,512]{2,1,0:T(8,128)(2,1)S(1)}, bf16[1,160,512]{2,1,0:T(8,128)(2,1)}, u32[]{:S(2)}) %copy-start.2) | copy-done | bytes 163864
  3.4 0.0 copy-start.3
  3.4 0.9 %copy-done.3 = bf16[1,160,512]{2,1,0:T(8,128)(2,1)S(1)} copy-done((bf16[1,160,512]{2,1,0:T(8,128)(2,1)S(1)}, bf16[1,160,512]{2,1,0:T(8,128)(2,1)}, u32[]{:S(2)}) %copy-start.3) | copy-done | bytes 163864
  4.4 0.0 copy-start.4
  4.4 0.7 %copy-done.4 = s32[1,160]{1,0:T(1,128)S(1)} copy-done((s32[1,160]{1,0:T(1,128)S(1)}, s32[1,160]{1,0:T(1,128)}, u32[]{:S(2)}) %copy-start.4) | copy-done | bytes 664
  5.0 47.6 %shard_map.101 = (bf16[1,160,1024]{2,1,0:T(8,128)(2,1)S(1)}, bf16[1,160,512]{2,1,0:T(8,128)(2,1)S(1)}, bf16[1,160,512]{2,1,0:T(8,128)(2,1)S(1)}, bf16[1,160,512]{2,1,0:T(8,128)(2,1)S(1)}, f32[512,512]{1,0:T(8,128)S(1)}) custom-call(bf16[1,160,512]{2,1,0:T(8,128)(2,1)S(1)} %copy-done.1, bf16[1,160,512]{2,1,0:T(8,128)(2,1)S(1)} %copy-done.2, ...), custom_call_target="tpu_custom_call" | custom-call | tf_op jit(solution)/shard_map/pallas_call | solution.py:417
  52.7 0.7 %copy.16 = bf16[1,160,1024]{2,1,0:T(8,128)(2,1)} copy(bf16[1,160,1024]{2,1,0:T(8,128)(2,1)S(1)} %get-tuple-element.10) | data formatting | bytes 655360
  53.4 0.7 %copy.17 = bf16[1,160,512]{2,1,0:T(8,128)(2,1)} copy(bf16[1,160,512]{2,1,0:T(8,128)(2,1)S(1)} %get-tuple-element.11) | data formatting | bytes 327680
  54.1 0.7 %copy.18 = bf16[1,160,512]{2,1,0:T(8,128)(2,1)} copy(bf16[1,160,512]{2,1,0:T(8,128)(2,1)S(1)} %get-tuple-element.12) | data formatting | bytes 327680
  54.7 0.7 %copy.19 = bf16[1,160,512]{2,1,0:T(8,128)(2,1)} copy(bf16[1,160,512]{2,1,0:T(8,128)(2,1)S(1)} %get-tuple-element.13) | data formatting | bytes 327680
  55.4 1.0 %copy.20 = f32[512,512]{1,0:T(8,128)} copy(f32[512,512]{1,0:T(8,128)S(1)} %get-tuple-element.14) | data formatting | bytes 2097152
Async XLA Ops:
  0.6 1.0 %copy-start = (bf16[1,160,1024]{2,1,0:T(8,128)(2,1)S(1)}, bf16[1,160,1024]{2,1,0:T(8,128)(2,1)}, u32[]{:S(2)}) copy-start(bf16[1,160,1024]{2,1,0:T(8,128)(2,1)} %cot_ref.1) | copy-start | bytes 983044
  1.6 0.9 %copy-start.1 = (bf16[1,160,512]{2,1,0:T(8,128)(2,1)S(1)}, bf16[1,160,512]{2,1,0:T(8,128)(2,1)}, u32[]{:S(2)}) copy-start(bf16[1,160,512]{2,1,0:T(8,128)(2,1)} %q_ref.1) | copy-start | bytes 491524
  2.5 0.9 %copy-start.2 = (bf16[1,160,512]{2,1,0:T(8,128)(2,1)S(1)}, bf16[1,160,512]{2,1,0:T(8,128)(2,1)}, u32[]{:S(2)}) copy-start(bf16[1,160,512]{2,1,0:T(8,128)(2,1)} %k_ref.1) | copy-start | bytes 491524
  3.4 0.9 %copy-start.3 = (bf16[1,160,512]{2,1,0:T(8,128)(2,1)S(1)}, bf16[1,160,512]{2,1,0:T(8,128)(2,1)}, u32[]{:S(2)}) copy-start(bf16[1,160,512]{2,1,0:T(8,128)(2,1)} %v_ref.1) | copy-start | bytes 491524
  4.4 0.7 %copy-start.4 = (s32[1,160]{1,0:T(1,128)S(1)}, s32[1,160]{1,0:T(1,128)}, u32[]{:S(2)}) copy-start(s32[1,160]{1,0:T(1,128)} %clip_ref.1) | copy-start | bytes 1924

commit v2 on v1

--- a/solution.py
+++ b/solution.py
@@ -21,12 +21,12 @@
 
 def fused_kernel(
     nd, nm, chunks,
-    q_ref, k_ref, v_ref, clip_ref, w_hbm, cot_ref,
+    q_hbm, k_hbm, v_hbm, clip_hbm, w_hbm, cot_hbm,
     mixed_ref, dq_ref, dk_ref, dv_ref, dw_ref,
-    w_ref, cot_full, cot_cols, att_all, kv_prev, clip_send, clip_prev,
+    q_ref, k_ref, v_ref, clip_ref, w_ref, cot_full, cot_cols, att_all, kv_prev, clip_send, clip_prev,
     p_own, p_prev, d_att, dkv_own, dkv_send, dkv_recv,
     up_out, up_in, down_out, down_in,
-    w_sem, own_sem, kv_ssem, kv_rsem, ag_up_ssem, ag_dn_ssem, ag_rsem,
+    in_sem, w_sem, own_sem, kv_ssem, kv_rsem, ag_up_ssem, ag_dn_ssem, ag_rsem,
     cc_ssem, cc_rsem, at_ssem, at_rsem,
     up_ssem, up_rsem, dn_ssem, dn_rsem, dkv_ssem, dkv_rsem,
 ):
@@ -37,7 +37,7 @@
     rows, width = q_ref.shape[1], q_ref.shape[2]
     heads = width // HD
     scale = HD ** (-0.5)
-    piece = cot_ref.shape[2]
+    piece = cot_full.shape[2]
     half = piece // nb
     part = piece // chunks
 
@@ -48,6 +48,15 @@
         )
 
     w_copy = pltpu.make_async_copy(w_hbm, w_ref, w_sem)
+    fetches = [
+        pltpu.make_async_copy(src, dst, in_sem.at[i])
+        for i, (src, dst) in enumerate((
+            (cot_hbm.at[0], cot_full.at[m]), (k_hbm, k_ref), (v_hbm, v_ref), (q_hbm, q_ref),
+            (clip_hbm, clip_ref),
+        ))
+    ]
+    for copy in fetches:
+        copy.start()
     w_copy.start()
 
     barrier = pltpu.get_barrier_semaphore()
@@ -66,8 +75,9 @@
         pl.semaphore_signal(barrier, inc=1, device_id=(d, b, m + 1), device_id_type=MESH)
 
     clip_send[...] = jnp.zeros_like(clip_send)
+    for copy in fetches:
+        copy.wait()
     clip_send[0:1, 0:rows] = clip_ref[...]
-    cot_full[m] = cot_ref[0]
     pl.semaphore_wait(
         barrier, group - 1 + jnp.where(m > 0, 1, 0) + jnp.where(m < nm - 1, 1, 0)
     )
@@ -131,7 +141,9 @@
         for copy in kv_copies():
             copy.start()
 
-    each_column(m, start, start)
+    @pl.when(b == 1)
+    def _():
+        each_column(m, start, start)
 
     def gather_step(step):
         @pl.when(m - step >= 0)
@@ -159,61 +171,95 @@
     row = lax.broadcasted_iota(jnp.int32, (rows, rows), 0)
     col = lax.broadcasted_iota(jnp.int32, (rows, rows), 1)
 
-    def clip_masks(use_prev):
-        here = jnp.broadcast_to(clip_send[0:1, 0:rows], (rows, rows))
-        mine = jnp.sum(jnp.where(row == col, here, 0), axis=1, keepdims=True)
-        own = jnp.logical_and(col <= row, here == mine)
-        prev = None
-        if use_prev:
-            prev = jnp.broadcast_to(clip_prev[0:1, 0:rows], (rows, rows)) == mine
-        return own, prev
-
-    def forward(use_prev):
-        own, prev = clip_masks(use_prev)
+    def clip_rows(ref):
+        return jnp.broadcast_to(ref[0:1, 0:rows], (rows, rows))
+
+    def own_scores(h):
+        cols = pl.ds(h * HD, HD)
+        return jnp.where(seen, dot(q_ref[0, :, cols], k_ref[0, :, cols], NT) * scale, NEG)
+
+    here = clip_rows(clip_send)
+    mine = jnp.sum(jnp.where(row == col, here, 0), axis=1, keepdims=True)
+    seen = jnp.logical_and(col <= row, here == mine)
+
+    @pl.when(b == 0)
+    def _():
         for h in range(heads):
             cols = pl.ds(h * HD, HD)
-            q = q_ref[0, :, cols]
-            s = jnp.where(own, dot(q, k_ref[0, :, cols], NT) * scale, NEG)
-            peak = jnp.max(s, axis=1, keepdims=True)
-            if use_prev:
-                t = jnp.where(prev, dot(q, kv_prev[0, :, cols], NT) * scale, NEG)
-                peak = jnp.maximum(peak, jnp.max(t, axis=1, keepdims=True))
-            e = jnp.exp(s - peak)
-            total = jnp.sum(e, axis=1, keepdims=True)
-            if use_prev:
-                f = jnp.exp(t - peak)
-                total = total + jnp.sum(f, axis=1, keepdims=True)
-            inverse = 1.0 / total
-            e = e * inverse
+            s = own_scores(h)
+            e = jnp.exp(s - jnp.max(s, axis=1, keepdims=True))
+            e = e * (1.0 / jnp.sum(e, axis=1, keepdims=True))
             p_own[h] = e
             att = dot(e.astype(jnp.bfloat16), v_ref[0, :, cols], NN)
-            if use_prev:
-                f = f * inverse
-                p_prev[h] = f
-                att = att + dot(f.astype(jnp.bfloat16), kv_prev[1, :, cols], NN)
             att_all[me, :, cols] = att.astype(jnp.bfloat16)
 
+    @pl.when(b == 1)
+    def _():
+        for h in range(heads):
+            p_own[h] = own_scores(h)
+
+    gather_step(1)
+
     @pl.when(b == 0)
     def _():
-        forward(False)
-
-    gather_step(1)
+        each_column(m, start, start)
 
     @pl.when(b == 1)
     def _():
-        for copy in kv_copies():
-            copy.wait_recv()
-        forward(True)
+        k_copy, v_copy, clip_copy = kv_copies()
+        clip_copy.wait_recv()
+        k_copy.wait_recv()
+        earlier = clip_rows(clip_prev) == mine
+        for h in range(heads):
+            cols = pl.ds(h * HD, HD)
+            s = p_own[h]
+            t = jnp.where(
+                earlier, dot(q_ref[0, :, cols], kv_prev[0, :, cols], NT) * scale, NEG
+            )
+            peak = jnp.maximum(
+                jnp.max(s, axis=1, keepdims=True), jnp.max(t, axis=1, keepdims=True)
+            )
+            e, f = jnp.exp(s - peak), jnp.exp(t - peak)
+            inverse = 1.0 / (
+                jnp.sum(e, axis=1, keepdims=True) + jnp.sum(f, axis=1, keepdims=True)
+            )
+            e, f = e * inverse, f * inverse
+            p_own[h] = e
+            p_prev[h] = f
+            dkv_own[0, :, cols] = dot(e.astype(jnp.bfloat16), v_ref[0, :, cols], NN)
+        v_copy.wait_recv()
+        for h in range(heads):
+            cols = pl.ds(h * HD, HD)
+            att = dkv_own[0, :, cols] + dot(
+                p_prev[h].astype(jnp.bfloat16), kv_prev[1, :, cols], NN
+            )
+            att_all[me, :, cols] = att.astype(jnp.bfloat16)
+
+    pairs = group // 2
+    core = lax.rem(d, 2)
+    partner = (d + 1 - 2 * core, b, m)
+    pair = (d // 2) * nb + b
+
+    def att_slot(off):
+        other = lax.rem(pair + off, pairs)
+        return (other // nb) * 2 + core, lax.rem(other, nb)
 
     def att_copy(off):
-        other = lax.rem(me + off, group)
+        to_d, to_b = att_slot(off)
         return remote(
-            att_all.at[me], att_all.at[me], at_ssem.at[off], at_rsem.at[me],
-            (other // nb, lax.rem(other, nb), m),
-        )
-
-    for off in range(1, group):
+            att_all.at[me], att_all.at[me], at_ssem.at[off], at_rsem.at[me], (to_d, to_b, m)
+        )
+
+    def att_pass(off):
+        of_d, of_b = att_slot(off)
+        slot = of_d * nb + of_b
+        return remote(
+            att_all.at[slot], att_all.at[slot], at_ssem.at[pairs + off], at_rsem.at[slot], partner
+        )
+
+    for off in range(1, pairs):
         att_copy(off).start()
+    att_pass(0).start()
 
     w_copy.wait()
 
@@ -321,14 +367,20 @@
 
     chain_step(nm - 2)
 
+    for off in range(1, pairs):
+        att_pass(off).wait_recv()
+        att_pass(off).start()
+
+    for off in range(pairs):
+        of_d, of_b = att_slot(off)
+        slot = (of_d + 1 - 2 * core) * nb + of_b
+        remote(
+            att_all.at[slot], att_all.at[slot], at_ssem.at[0], at_rsem.at[slot], partner
+        ).wait_recv()
     for off in range(1, group):
         other = lax.rem(me + off, group)
-        peer = (other // nb, lax.rem(other, nb), m)
         remote(
-            att_all.at[other], att_all.at[other], at_ssem.at[off], at_rsem.at[other], peer
-        ).wait_recv()
-        remote(
-            cot_cols.at[other], cot_cols.at[other], cc_ssem.at[0, 0], cc_rsem.at[other], peer
+            cot_cols.at[other], cot_cols.at[other], cc_ssem.at[0, 0], cc_rsem.at[other], partner
         ).wait_recv()
     own_copy(0).wait()
     dw_ref[...] = dot(
@@ -390,8 +442,10 @@
             def _():
                 sum_down(shard, c).wait_send()
 
-    for off in range(1, group):
+    for off in range(1, pairs):
         att_copy(off).wait_send()
+    for off in range(pairs):
+        att_pass(off).wait_send()
 
     @pl.when(b == 0)
     def _():
@@ -401,6 +455,15 @@
     @pl.when(b == 1)
     def _():
         dkv_copy().wait_send()
+
+
+def write_kernel(*refs):
+    sem = refs[10]
+    copies = [pltpu.make_async_copy(refs[i], refs[5 + i], sem.at[i]) for i in range(5)]
+    for copy in copies:
+        copy.start()
+    for copy in copies:
+        copy.wait()
 
 
 def fused(nd, nm, queries, keys, values, clip_ids, w_out, cotangent):
@@ -414,7 +477,7 @@
     bf16, f32 = jnp.bfloat16, jnp.float32
     dma = pltpu.SemaphoreType.DMA
     vmem = pl.BlockSpec(memory_space=pltpu.VMEM)
-    return pl.pallas_call(
+    results = pl.pallas_call(
         functools.partial(fused_kernel, nd, nm, chunks),
         out_shape=(
             jax.ShapeDtypeStruct((1, rows, piece), bf16),
@@ -423,9 +486,13 @@
             jax.ShapeDtypeStruct((1, rows, width), bf16),
             jax.ShapeDtypeStruct((width, half), f32),
         ),
-        in_specs=[vmem] * 4 + [pl.BlockSpec(memory_space=pl.ANY), vmem],
+        in_specs=[pl.BlockSpec(memory_space=pltpu.HBM)] * 6,
         out_specs=(vmem,) * 5,
         scratch_shapes=[
+            pltpu.VMEM(queries.shape, bf16),
+            pltpu.VMEM(queries.shape, bf16),
+            pltpu.VMEM(queries.shape, bf16),
+            pltpu.VMEM(clip_ids.shape, jnp.int32),
             pltpu.VMEM(w_out.shape, bf16),
             pltpu.VMEM((nm, rows, piece), bf16),
             pltpu.VMEM((group, rows, half), bf16),
@@ -443,14 +510,22 @@
             pltpu.VMEM((nm, chunks, rows, part), bf16),
             pltpu.VMEM((nm, chunks, rows, part), bf16),
             pltpu.VMEM((nm, chunks, rows, part), bf16),
-            dma, dma, dma((3,)), dma((3,)), dma((nm,)), dma((nm,)), dma((nm,)),
+            dma((5,)), dma, dma, dma((3,)), dma((3,)), dma((nm,)), dma((nm,)), dma((nm,)),
             dma((nm, nb)), dma((group,)), dma((group,)), dma((group,)),
             dma((nm, chunks)), dma((nm, chunks)), dma((nm, chunks)), dma((nm, chunks)), dma, dma,
         ],
         compiler_params=pltpu.CompilerParams(
-            collective_id=0, has_side_effects=True, vmem_limit_bytes=48 * 1024 * 1024
+            collective_id=0, has_side_effects=True, vmem_limit_bytes=61 * 1024 * 1024
         ),
     )(queries, keys, values, clip_ids, w_out, cotangent)
+    return pl.pallas_call(
+        write_kernel,
+        out_shape=tuple(jax.ShapeDtypeStruct(x.shape, x.dtype) for x in results),
+        in_specs=[pl.BlockSpec(memory_space=pltpu.HBM)] * 5,
+        out_specs=(pl.BlockSpec(memory_space=pltpu.HBM),) * 5,
+        scratch_shapes=[dma((5,))],
+        compiler_params=pltpu.CompilerParams(vmem_limit_bytes=61 * 1024 * 1024),
+    )(*results)
 
 
 def seen_mask(q_pos, q_clip, k_pos, k_clip):
@@ -575,7 +650,7 @@
     )
     nd, nb, nm = mesh.shape["dp"], mesh.shape["blk"], mesh.shape["mp"]
     body = per_device
-    if nb == 2 and nd == nm:
+    if nb == 2 and nd == nm and nd % 2 == 0:
         body = functools.partial(fused, nd, nm)
     return jax.shard_map(
         body,

time: 56.6 us -> 104 us (1.84)
  Pallas kernels: 47.6 us -> 104 us
  local copies, waits for them, and re-layouts: 8.08 us -> 0 us
    pallas_call x0 -> x1, Pallas kernels: none -> 57.7 us  [fused(): pl.pallas_call(write_kernel, out_shape=tuple((jax.ShapeDtypeStruct(x.shap...]
    unnamed x15 -> x0, local copies, waits for them, and re-layouts: 8.08 us -> none
    pallas_call x1, Pallas kernels: 47.6 us -> 45.9 us  [fused(): pl.pallas_call(functools.partial(fused_kernel, nd, nm, chunks), out_shape...]
where the time goes in v2:
time: 104 us
  Pallas kernels  104 us (100%)
    pallas_call x1, Pallas kernels, fused(): pl.pallas_call(write_kernel, out_shape=tuple((jax.ShapeDtypeStruct(x.shap...  57.7 us
    pallas_call x1, Pallas kernels, fused(): pl.pallas_call(functools.partial(fused_kernel, nd, nm, chunks), out_shape...  45.9 us

profile of v2, /device:TPU:0, one launch (start us, length us, event | category | flops | bytes accessed | tf_op | source)
XLA Modules:
  0.0 104.3 jit_solution(2647570556084532586)
XLA Ops:
  0.6 45.9 %shard_map.101 = (bf16[1,160,1024]{2,1,0:T(8,128)(2,1)}, bf16[1,160,512]{2,1,0:T(8,128)(2,1)}, bf16[1,160,512]{2,1,0:T(8,128)(2,1)}, bf16[1,160,512]{2,1,0:T(8,128)(2,1)}, f32[512,512]{1,0:T(8,128)}) custom-call(bf16[1,160,512]{2,1,0:T(8,128)(2,1)} %q_hbm.1, bf16[1,160,512]{2,1,0:T(8,128)(2,1)} %k_hbm.1, bf16[1,160,512]{2,1,0:T(8,128)(2,1)} %v_hbm.1, ...), custom_call_target="tpu_custom_call" | custom-call | tf_op jit(solution)/shard_map/pallas_call | solution.py:480
  46.6 57.7 %shard_map.102 = (bf16[1,160,1024]{2,1,0:T(8,128)(2,1)}, bf16[1,160,512]{2,1,0:T(8,128)(2,1)}, bf16[1,160,512]{2,1,0:T(8,128)(2,1)}, bf16[1,160,512]{2,1,0:T(8,128)(2,1)}, f32[512,512]{1,0:T(8,128)}) custom-call(bf16[1,160,1024]{2,1,0:T(8,128)(2,1)} %get-tuple-element.10.refs_0_, bf16[1,160,512]{2,1,0:T(8,128)(2,1)} %get-tuple-element.11.refs_1_, ...), custom_call_target="tpu_custom_call" | custom-call | tf_op jit(solution)/shard_map/pallas_call | solution.py:521

commit v3 on v2

--- a/solution.py
+++ b/solution.py
@@ -22,7 +22,8 @@
 def fused_kernel(
     nd, nm, chunks,
     q_hbm, k_hbm, v_hbm, clip_hbm, w_hbm, cot_hbm,
-    mixed_ref, dq_ref, dk_ref, dv_ref, dw_ref,
+    mixed_hbm, dq_hbm, dk_hbm, dv_hbm, dw_hbm,
+    mixed_ref, dq_ref, dk_ref, dv_ref, dw_ref, out_sem,
     q_ref, k_ref, v_ref, clip_ref, w_ref, cot_full, cot_cols, att_all, kv_prev, clip_send, clip_prev,
     p_own, p_prev, d_att, dkv_own, dkv_send, dkv_recv,
     up_out, up_in, down_out, down_in,
@@ -365,6 +366,15 @@
         backward(True)
         dkv_copy().start()
 
+    stores = [
+        pltpu.make_async_copy(src, dst, out_sem.at[i])
+        for i, (src, dst) in enumerate((
+            (mixed_ref, mixed_hbm), (dq_ref, dq_hbm), (dk_ref, dk_hbm), (dv_ref, dv_hbm),
+            (dw_ref, dw_hbm),
+        ))
+    ]
+    stores[1].start()
+
     chain_step(nm - 2)
 
     for off in range(1, pairs):
@@ -387,12 +397,17 @@
         att_all[...].reshape(group * rows, width), cot_cols[...].reshape(group * rows, half), TN
     )
 
+    stores[4].start()
+
     @pl.when(b == 0)
     def _():
         dkv_copy().wait_recv()
         dk_ref[0] = (dkv_own[0] + dkv_recv[0].astype(jnp.float32)).astype(jnp.bfloat16)
         dv_ref[0] = (dkv_own[1] + dkv_recv[1].astype(jnp.float32)).astype(jnp.bfloat16)
 
+    stores[2].start()
+    stores[3].start()
+
     for c in range(chunks):
         mine = partial(m, c)
         at = slice(c * part, (c + 1) * part)
@@ -418,6 +433,8 @@
             mixed_ref[0, :, at] = (
                 mine + up_in[m, c].astype(jnp.float32) + down_in[m, c].astype(jnp.float32)
             ).astype(jnp.bfloat16)
+
+    stores[0].start()
 
     for shard in range(nm):
         @pl.when(jnp.logical_and(m < nm - 1, shard <= m))
@@ -456,13 +473,21 @@
     def _():
         dkv_copy().wait_send()
 
+    for copy in stores:
+        copy.wait()
+
 
 def write_kernel(*refs):
-    sem = refs[10]
-    copies = [pltpu.make_async_copy(refs[i], refs[5 + i], sem.at[i]) for i in range(5)]
-    for copy in copies:
+    sources, results, held = refs[:5], refs[5:10], refs[10:15]
+    in_sem, out_sem = refs[15:]
+    reads = [pltpu.make_async_copy(sources[i], held[i], in_sem.at[i]) for i in range(5)]
+    writes = [pltpu.make_async_copy(held[i], results[i], out_sem.at[i]) for i in range(5)]
+    for copy in reads:
         copy.start()
-    for copy in copies:
+    for read, write in zip(reads, writes):
+        read.wait()
+        write.start()
+    for copy in writes:
         copy.wait()
 
 
@@ -476,7 +501,6 @@
     lanes = -(-rows // 128) * 128
     bf16, f32 = jnp.bfloat16, jnp.float32
     dma = pltpu.SemaphoreType.DMA
-    vmem = pl.BlockSpec(memory_space=pltpu.VMEM)
     results = pl.pallas_call(
         functools.partial(fused_kernel, nd, nm, chunks),
         out_shape=(
@@ -487,8 +511,14 @@
             jax.ShapeDtypeStruct((width, half), f32),
         ),
         in_specs=[pl.BlockSpec(memory_space=pltpu.HBM)] * 6,
-        out_specs=(vmem,) * 5,
+        out_specs=(pl.BlockSpec(memory_space=pltpu.HBM),) * 5,
         scratch_shapes=[
+            pltpu.VMEM((1, rows, piece), bf16),
+            pltpu.VMEM((1, rows, width), bf16),
+            pltpu.VMEM((1, rows, width), bf16),
+            pltpu.VMEM((1, rows, width), bf16),
+            pltpu.VMEM((width, half), f32),
+            dma((5,)),
             pltpu.VMEM(queries.shape, bf16),
             pltpu.VMEM(queries.shape, bf16),
             pltpu.VMEM(queries.shape, bf16),
@@ -523,7 +553,7 @@
         out_shape=tuple(jax.ShapeDtypeStruct(x.shape, x.dtype) for x in results),
         in_specs=[pl.BlockSpec(memory_space=pltpu.HBM)] * 5,
         out_specs=(pl.BlockSpec(memory_space=pltpu.HBM),) * 5,
-        scratch_shapes=[dma((5,))],
+        scratch_shapes=[pltpu.VMEM(x.shape, x.dtype) for x in results] + [dma((5,)), dma((5,))],
         compiler_params=pltpu.CompilerParams(vmem_limit_bytes=61 * 1024 * 1024),
     )(*results)
 

time: 104 us -> 48.8 us (0.47)
  Pallas kernels: 104 us -> 48 us
    pallas_call x1, Pallas kernels: 57.7 us -> 2.6 us  [fused(): pl.pallas_call(write_kernel, out_shape=tuple((jax.ShapeDtypeStruct(x.shap...]
where the time goes in v3:
time: 48.8 us; the launch traced here: 48.6 us
  Pallas kernels  48 us (98%)
  between operations  0.64 us (1%)
    pallas_call x1, Pallas kernels, fused(): pl.pallas_call(functools.partial(fused_kernel, nd, nm, chunks), out_shape...  45.4 us
    pallas_call x1, Pallas kernels, fused(): pl.pallas_call(write_kernel, out_shape=tuple((jax.ShapeDtypeStruct(x.shap...  2.6 us

profile of v3, /device:TPU:0, one launch (start us, length us, event | category | flops | bytes accessed | tf_op | source)
XLA Modules:
  0.0 48.6 jit_solution(9378592285766019677)
XLA Ops:
  0.6 45.4 %shard_map.101 = (bf16[1,160,1024]{2,1,0:T(8,128)(2,1)}, bf16[1,160,512]{2,1,0:T(8,128)(2,1)}, bf16[1,160,512]{2,1,0:T(8,128)(2,1)}, bf16[1,160,512]{2,1,0:T(8,128)(2,1)}, f32[512,512]{1,0:T(8,128)}) custom-call(bf16[1,160,512]{2,1,0:T(8,128)(2,1)} %q_hbm.1, bf16[1,160,512]{2,1,0:T(8,128)(2,1)} %k_hbm.1, bf16[1,160,512]{2,1,0:T(8,128)(2,1)} %v_hbm.1, ...), custom_call_target="tpu_custom_call" | custom-call | tf_op jit(solution)/shard_map/pallas_call | solution.py:504
  46.0 2.6 %shard_map.102 = (bf16[1,160,1024]{2,1,0:T(8,128)(2,1)}, bf16[1,160,512]{2,1,0:T(8,128)(2,1)}, bf16[1,160,512]{2,1,0:T(8,128)(2,1)}, bf16[1,160,512]{2,1,0:T(8,128)(2,1)}, f32[512,512]{1,0:T(8,128)}) custom-call(bf16[1,160,1024]{2,1,0:T(8,128)(2,1)} %get-tuple-element.10.refs_0_, bf16[1,160,512]{2,1,0:T(8,128)(2,1)} %get-tuple-element.11.refs_1_, ...), custom_call_target="tpu_custom_call" | custom-call | tf_op jit(solution)/shard_map/pallas_call | solution.py:551

commit v4 on v3

--- a/solution.py
+++ b/solution.py
@@ -318,8 +318,14 @@
 
                 sum_down(dest, c).start()
 
+    at_end = jnp.logical_or(m == 0, m == nm - 1)
     for step in range(nm - 2):
         chain_step(step)
+        if step == nm - 3:
+            @pl.when(at_end)
+            def _():
+                chain_step(nm - 2)
+
         gather_step(step + 2)
 
     total = dot(cot_full[0], w_ref[:, 0:piece], NT)
@@ -375,11 +381,13 @@
     ]
     stores[1].start()
 
-    chain_step(nm - 2)
-
     for off in range(1, pairs):
         att_pass(off).wait_recv()
         att_pass(off).start()
+
+    @pl.when(jnp.logical_not(at_end))
+    def _():
+        chain_step(nm - 2)
 
     for off in range(pairs):
         of_d, of_b = att_slot(off)
@@ -680,7 +688,7 @@
     )
     nd, nb, nm = mesh.shape["dp"], mesh.shape["blk"], mesh.shape["mp"]
     body = per_device
-    if nb == 2 and nd == nm and nd % 2 == 0:
+    if nb == 2 and nd == nm and nd % 2 == 0 and nd > 2:
         body = functools.partial(fused, nd, nm)
     return jax.shard_map(
         body,

time: 48.8 us -> 47.7 us (0.977)
  Pallas kernels: 48 us -> 47 us
    pallas_call x1, Pallas kernels: 45.4 us -> 44.4 us  [fused(): pl.pallas_call(functools.partial(fused_kernel, nd, nm, chunks), out_shape...]
where the time goes in v4:
time: 47.7 us; the launch traced here: 47.6 us
  Pallas kernels  47 us (99%)
  between operations  0.64 us (1%)
    pallas_call x1, Pallas kernels, fused(): pl.pallas_call(functools.partial(fused_kernel, nd, nm, chunks), out_shape...  44.4 us
    pallas_call x1, Pallas kernels, fused(): pl.pallas_call(write_kernel, out_shape=tuple((jax.ShapeDtypeStruct(x.shap...  2.6 us

profile of v4, /device:TPU:0, one launch (start us, length us, event | category | flops | bytes accessed | tf_op | source)
XLA Modules:
  0.0 47.6 jit_solution(18336846044201806641)
XLA Ops:
  0.6 44.4 %shard_map.101 = (bf16[1,160,1024]{2,1,0:T(8,128)(2,1)}, bf16[1,160,512]{2,1,0:T(8,128)(2,1)}, bf16[1,160,512]{2,1,0:T(8,128)(2,1)}, bf16[1,160,512]{2,1,0:T(8,128)(2,1)}, f32[512,512]{1,0:T(8,128)}) custom-call(bf16[1,160,512]{2,1,0:T(8,128)(2,1)} %q_hbm.1, bf16[1,160,512]{2,1,0:T(8,128)(2,1)} %k_hbm.1, bf16[1,160,512]{2,1,0:T(8,128)(2,1)} %v_hbm.1, ...), custom_call_target="tpu_custom_call" | custom-call | tf_op jit(solution)/shard_map/pallas_call | solution.py:512
  45.0 2.6 %shard_map.102 = (bf16[1,160,1024]{2,1,0:T(8,128)(2,1)}, bf16[1,160,512]{2,1,0:T(8,128)(2,1)}, bf16[1,160,512]{2,1,0:T(8,128)(2,1)}, bf16[1,160,512]{2,1,0:T(8,128)(2,1)}, f32[512,512]{1,0:T(8,128)}) custom-call(bf16[1,160,1024]{2,1,0:T(8,128)(2,1)} %get-tuple-element.10.refs_0_, bf16[1,160,512]{2,1,0:T(8,128)(2,1)} %get-tuple-element.11.refs_1_, ...), custom_call_target="tpu_custom_call" | custom-call | tf_op jit(solution)/shard_map/pallas_call | solution.py:559

commit v5 on v4

--- a/solution.py
+++ b/solution.py
@@ -389,21 +389,27 @@
     def _():
         chain_step(nm - 2)
 
-    for off in range(pairs):
-        of_d, of_b = att_slot(off)
-        slot = (of_d + 1 - 2 * core) * nb + of_b
+    def arrived(buffer, slot, sems):
         remote(
-            att_all.at[slot], att_all.at[slot], at_ssem.at[0], at_rsem.at[slot], partner
+            buffer.at[slot], buffer.at[slot], at_ssem.at[0], sems.at[slot], partner
         ).wait_recv()
-    for off in range(1, group):
-        other = lax.rem(me + off, group)
-        remote(
-            cot_cols.at[other], cot_cols.at[other], cc_ssem.at[0, 0], cc_rsem.at[other], partner
-        ).wait_recv()
-    own_copy(0).wait()
-    dw_ref[...] = dot(
-        att_all[...].reshape(group * rows, width), cot_cols[...].reshape(group * rows, half), TN
-    )
+
+    for off in range(nd):
+        first = lax.rem(d + off, nd) * nb
+        if off == 0:
+            own_copy(0).wait()
+            arrived(cot_cols, first + 1 - b, cc_rsem)
+        else:
+            for to_b in range(nb):
+                arrived(cot_cols, first + to_b, cc_rsem)
+        if off % 2 == 1:
+            for to_b in range(nb):
+                arrived(att_all, first + to_b, at_rsem)
+        grad = dot(
+            att_all[pl.ds(first, nb)].reshape(nb * rows, width),
+            cot_cols[pl.ds(first, nb)].reshape(nb * rows, half), TN,
+        )
+        dw_ref[...] = grad if off == 0 else dw_ref[...] + grad
 
     stores[4].start()
 
@@ -490,6 +496,7 @@
     in_sem, out_sem = refs[15:]
     reads = [pltpu.make_async_copy(sources[i], held[i], in_sem.at[i]) for i in range(5)]
     writes = [pltpu.make_async_copy(held[i], results[i], out_sem.at[i]) for i in range(5)]
+    reads, writes = reads[::-1], writes[::-1]
     for copy in reads:
         copy.start()
     for read, write in zip(reads, writes):

time: 47.7 us -> 47.7 us (level)
  no operation moved by 1% of the time
where the time goes in v5:
time: 47.7 us; the launch traced here: 47.5 us
  Pallas kernels  46.9 us (98%)
  between operations  0.64 us (1%)
    pallas_call x1, Pallas kernels, fused(): pl.pallas_call(functools.partial(fused_kernel, nd, nm, chunks), out_shape...  44.4 us
    pallas_call x1, Pallas kernels, fused(): pl.pallas_call(write_kernel, out_shape=tuple((jax.ShapeDtypeStruct(x.shap...  2.54 us

profile of v5, /device:TPU:0, one launch (start us, length us, event | category | flops | bytes accessed | tf_op | source)
XLA Modules:
  0.0 47.5 jit_solution(13063712538805943883)
XLA Ops:
  0.6 44.4 %shard_map.101 = (bf16[1,160,1024]{2,1,0:T(8,128)(2,1)}, bf16[1,160,512]{2,1,0:T(8,128)(2,1)}, bf16[1,160,512]{2,1,0:T(8,128)(2,1)}, bf16[1,160,512]{2,1,0:T(8,128)(2,1)}, f32[512,512]{1,0:T(8,128)}) custom-call(bf16[1,160,512]{2,1,0:T(8,128)(2,1)} %q_hbm.1, bf16[1,160,512]{2,1,0:T(8,128)(2,1)} %k_hbm.1, bf16[1,160,512]{2,1,0:T(8,128)(2,1)} %v_hbm.1, ...), custom_call_target="tpu_custom_call" | custom-call | tf_op jit(solution)/shard_map/pallas_call | solution.py:519
  45.0 2.5 %shard_map.102 = (bf16[1,160,1024]{2,1,0:T(8,128)(2,1)}, bf16[1,160,512]{2,1,0:T(8,128)(2,1)}, bf16[1,160,512]{2,1,0:T(8,128)(2,1)}, bf16[1,160,512]{2,1,0:T(8,128)(2,1)}, f32[512,512]{1,0:T(8,128)}) custom-call(bf16[1,160,1024]{2,1,0:T(8,128)(2,1)} %get-tuple-element.10.refs_0_, bf16[1,160,512]{2,1,0:T(8,128)(2,1)} %get-tuple-element.11.refs_1_, ...), custom_call_target="tpu_custom_call" | custom-call | tf_op jit(solution)/shard_map/pallas_call | solution.py:566
